TPU v7x, 32 devices: a whole 2x2x4 slice. The times are simulated.
32 devices in a mesh: dom: 2 (over y), row: 4 (over x, core), col: 4 (over z).
Axes of the slice: x: 2, y: 2, z: 4, core: 2. Of those that a mesh axis runs over, the one named last changes fastest.
Arguments:
- ext_ext: float32 [4, 2304, 2304], P('dom', 'row', 'col'), parts along dimension 0, may hold values from -0.125 to 0.125
- ext_int: float32 [4, 2304, 768], P('dom', 'row', 'col'), parts along dimension 0, may hold values from -0.21875 to 0.21875
- int_ext: float32 [4, 768, 2304], P('dom', 'row', 'col'), parts along dimension 0, may hold values from -0.125 to 0.125
- int_int: float32 [4, 768, 768], P('dom', 'row', 'col'), parts along dimension 0, may hold values from -2 to 2, as said below
- boundary_data: float32 [4, 2304, 128], P('dom', 'row', 'col'), parts along dimension 0, may hold values from -6 to 6
- leaf_ext_ext: float32 [32, 2, 576, 576], P(('dom', 'row', 'col')), parts along dimension 0, may hold values from -0.25 to 0.25
- leaf_ext_int: float32 [32, 2, 576, 192], P(('dom', 'row', 'col')), parts along dimension 0, may hold values from -0.4375 to 0.4375
- leaf_int_ext: float32 [32, 2, 192, 576], P(('dom', 'row', 'col')), parts along dimension 0, may hold values from -0.25 to 0.25
- leaf_int_int: float32 [32, 2, 192, 192], P(('dom', 'row', 'col')), parts along dimension 0, may hold values from -2 to 2, as said below
Outputs:
- parent_map: float32 [4, 2, 2304, 2304], P('dom', None, 'row', 'col'), parts along dimension 0
- solve_op: float32 [4, 768, 2304], P('dom', 'row', 'col'), parts along dimension 0
- interface_values: float32 [1536, 128], P(('dom', 'row'), 'col'), parts along dimension 0
- leaf_parent: float32 [32, 2, 2, 576, 576], P(('dom', 'row', 'col')), parts along dimension 0
- leaf_solve: float32 [32, 2, 192, 576], P(('dom', 'row', 'col')), parts along dimension 0
There are 2 independent parts, one for each index of `dom`. A program takes and returns all parts, laid end to end along the dimension named above; each array names one. Nothing has to cross between parts.
Inputs may be any that keep to these rules, and one draw needn't show every extreme that they name: `int_int`: off-diagonal entries are small against a diagonal between 1 and 2 in each child's map. `leaf_int_int`: off-diagonal entries are small against a diagonal between 1 and 2 in each child's map.
All inputs are finite; a program needn't handle non-finite values.
Results may differ from a plain program's by a relative error of at most 0.00022.
Values sent between devices are 32-bit elements; how exact they have to be, the bound alone decides.
A program may use at most 128 MiB of HBM per device.

v0:
```python
import jax
import jax.numpy as jnp
from jax import lax
from jax.sharding import PartitionSpec as P

ITERS = 2


def matmul(a, b):
    return jnp.dot(a, b, precision=lax.Precision.HIGHEST, preferred_element_type=jnp.float32)


def panel(block):
    return lax.all_gather(block, "col", axis=1, tiled=True)


def fold_product(left_rows, right_block):
    return matmul(left_rows, lax.all_gather(right_block, "row", axis=0, tiled=True))


def product(left_block, right_block):
    return fold_product(panel(left_block), right_block)


def merge_local(ee, ei, ie, ii):
    side = ii.shape[1]
    third = ee.shape[1]
    joint = ii[0] + ii[1]
    eye = jnp.eye(side, dtype=jnp.float32)
    current = eye / jnp.diagonal(joint)[None, :]
    for step in range(ITERS):
        current = 2.0 * current - matmul(current, matmul(joint, current))
    coupling = jnp.concatenate([ie[0], ie[1]], axis=1)
    solution = -matmul(current, coupling)
    solve = jnp.stack([solution[:, :third], solution[:, third:]])
    lifted = matmul(ei.reshape(2 * third, side), solution)
    lifted = lifted.reshape(2, third, 2, third).transpose(0, 2, 1, 3)
    pairs = jnp.eye(2, dtype=jnp.float32)
    parent = lifted + pairs[:, :, None, None] * ee[:, None]
    return (parent, solve)


def shards(
    ext_ext,
    ext_int,
    int_ext,
    int_int,
    boundary_data,
    leaf_ext_ext,
    leaf_ext_int,
    leaf_int_ext,
    leaf_int_int,
):
    n_col = lax.axis_size("col")
    joint = int_int[0] + int_int[1]
    rows_here = joint.shape[0]
    cols_here = joint.shape[1]
    third = ext_ext.shape[2]
    coupling = jnp.concatenate([int_ext[0], int_ext[1]], axis=1)
    global_row = lax.axis_index("row") * rows_here + lax.broadcasted_iota(jnp.int32, joint.shape, 0)
    global_col = lax.axis_index("col") * cols_here + lax.broadcasted_iota(jnp.int32, joint.shape, 1)
    on_diag = global_row == global_col
    current = jnp.where(on_diag, 1.0 / jnp.where(on_diag, joint, 1.0), 0.0)
    for step in range(ITERS):
        current = 2.0 * current - product(current, product(joint, current))
    solution = -product(current, coupling)
    leaf_parent, leaf_solve = jax.vmap(merge_local)(
        leaf_ext_ext, leaf_ext_int, leaf_int_ext, leaf_int_int
    )
    solve_op = jnp.stack([solution[:, :third], solution[:, third:]])
    ext_rows = ext_int.shape[1]
    lifted = product(ext_int.reshape(2 * ext_rows, ext_int.shape[2]), solution)
    lifted = lifted.reshape(2, ext_rows, 2, third).transpose(0, 2, 1, 3)
    pairs = jnp.eye(2, dtype=jnp.float32)
    parent_map = lifted + pairs[:, :, None, None] * ext_ext[:, None]
    operator_rows = panel(solution)
    operator_rows = operator_rows.reshape(rows_here, n_col, 2, third).transpose(0, 2, 1, 3)
    operator_rows = operator_rows.reshape(rows_here, 2, n_col * third)
    interface_values = jnp.einsum(
        "pcn,cnq->pq",
        operator_rows,
        lax.all_gather(boundary_data, "row", axis=1, tiled=True),
        precision=lax.Precision.HIGHEST,
    )
    return (parent_map, solve_op, interface_values, leaf_parent, leaf_solve)


def solution(mesh):
    in_specs = (
        P("dom", "row", "col"),
        P("dom", "row", "col"),
        P("dom", "row", "col"),
        P("dom", "row", "col"),
        P("dom", "row", "col"),
        P(("dom", "row", "col"), None, None, None),
        P(("dom", "row", "col"), None, None, None),
        P(("dom", "row", "col"), None, None, None),
        P(("dom", "row", "col"), None, None, None),
    )
    out_specs = (
        P("dom", None, "row", "col"),
        P("dom", "row", "col"),
        P(("dom", "row"), "col"),
        P(("dom", "row", "col"), None, None, None, None),
        P(("dom", "row", "col"), None, None, None),
    )
    return jax.shard_map(shards, mesh=mesh, in_specs=in_specs, out_specs=out_specs, check_vma=False)
```

profile of v0, /device:TPU:0, one launch (start us, length us, event | category | flops | bytes accessed | tf_op | source)
XLA Modules:
  0.0 292.4 jit_solution(13432274406782789634)
XLA Ops:
  7.2 1.4 slice_bitcast_fusion.7
  8.6 1.1 pad_maximum_fusion.1
  10.6 1.6 reshape.154
  12.6 21.3 %all-gather = f32[1,192,768]{1,0,2:T(1,128)S(1)} all-gather(f32[1,192,192]{1,0,2:T(1,128)S(1)} %copy.41), channel_id=2, replica_groups=mesh['dom'=2,'row'=4,'col'=4] {'col'}, dimensions={2}, use_global_device_ids=true | all-gather | bytes 737280 | tf_op jit(solution)/shard_map/all_gather | solution.py:14
  34.4 12.8 %all_gather.42 = f32[768,192]{1,0:T(8,128)S(1)} all-gather(f32[192,192]{1,0:T(8,128)S(1)} %get-tuple-element.25), channel_id=1, replica_groups=mesh['dom'=2,'row'=4,'col'=4] {'row'}, dimensions={0}, use_global_device_ids=true | all-gather | bytes 737280 | tf_op jit(solution)/shard_map/all_gather | solution.py:18
  47.2 21.7 %all_gather.40 = f32[192,768]{0,1:T(8,128)S(1)} all-gather(f32[192,192]{0,1:T(8,128)S(1)} %copy.40), channel_id=1, replica_groups=mesh['dom'=2,'row'=4,'col'=4] {'col'}, dimensions={1}, use_global_device_ids=true | all-gather | bytes 737280 | tf_op jit(solution)/shard_map/all_gather | solution.py:14
  69.5 7.9 %all_gather.43 = f32[768,192]{1,0:T(8,128)S(1)} all-gather(f32[192,192]{1,0:T(8,128)S(1)} %fusion.11), channel_id=1, replica_groups=mesh['dom'=2,'row'=4,'col'=4] {'row'}, dimensions={0}, use_global_device_ids=true | all-gather | bytes 737280 | tf_op jit(solution)/shard_map/all_gather | solution.py:18
  77.4 1.4 convolution_subtract_fusion.3
  78.9 8.7 %all_gather.45 = f32[768,192]{1,0:T(8,128)S(1)} all-gather(f32[192,192]{1,0:T(8,128)S(1)} %convolution_subtract_fusion.3), channel_id=1, replica_groups=mesh['dom'=2,'row'=4,'col'=4] {'row'}, dimensions={0}, use_global_device_ids=true | all-gather | bytes 737280 | tf_op jit(solution)/shard_map/all_gather | solution.py:18
  87.6 30.7 %all_gather.44 = f32[192,768]{0,1:T(8,128)S(1)} all-gather(f32[192,192]{0,1:T(8,128)S(1)} %copy.43), channel_id=1, replica_groups=mesh['dom'=2,'row'=4,'col'=4] {'col'}, dimensions={1}, use_global_device_ids=true | all-gather | bytes 737280 | tf_op jit(solution)/shard_map/all_gather | solution.py:14
  119.0 8.4 %all_gather.46 = f32[768,192]{1,0:T(8,128)S(1)} all-gather(f32[192,192]{1,0:T(8,128)S(1)} %fusion.9), channel_id=1, replica_groups=mesh['dom'=2,'row'=4,'col'=4] {'row'}, dimensions={0}, use_global_device_ids=true | all-gather | bytes 737280 | tf_op jit(solution)/shard_map/all_gather | solution.py:18
  127.4 1.4 convolution_subtract_fusion.2
  129.0 20.8 %all_gather.47 = f32[192,768]{0,1:T(8,128)S(1)} all-gather(f32[192,192]{0,1:T(8,128)S(1)} %copy.44), channel_id=1, replica_groups=mesh['dom'=2,'row'=4,'col'=4] {'col'}, dimensions={1}, use_global_device_ids=true | all-gather | bytes 737280 | tf_op jit(solution)/shard_map/all_gather | solution.py:14
  149.7 5.6 %convolution_negate_fusion.1 = f32[192,1152]{1,0:T(8,128)} fusion(f32[192,768]{0,1:T(8,128)S(1)} %all_gather.47, f32[768,1152]{1,0:T(8,128)} %all-gather.6.cloned.1.call-done), kind=kOutput, calls=%fused_computation.5 | convolution fusion | flops 2038652928 | bytes 5013504 | tf_op jit(solution)/shard_map/dot_general | solution.py:10
  156.0 1.0 copy.49
  157.1 3.5 %copy.52 = f32[2,576,576]{1,2,0:T(8,128)} copy(f32[2,576,576]{2,1,0:T(8,128)} %bitcast.83) | data formatting | bytes 5308416 | tf_op jit(solution)/shard_map/vmap()/mul | solution.py:39
  160.6 1.9 gather_fusion
  163.9 1.0 convolution_negate_fusion
  165.6 9.5 %bitcast_add_fusion = f32[1,2,2,576,576]{3,4,1,2,0:T(8,128)} fusion(f32[2,576,576]{1,2,0:T(8,128)} %copy.52, f32[2,2]{0,1:T(2,128)S(1)} %compare_convert_fusion, f32[1,2,576,192]{2,3,1,0:T(8,128)S(1)} %copy-done, f32[2,576,192,1]{1,0,2,3:T(2,128)S(1)} %bitcast.82), kind=kOutput, calls=%fused_computation.2 | convolution fusion | flops 3060301824 | bytes 9732112 | tf_op jit(solution)/shard_map/vmap()/dot_general | solution.py:10
  175.1 6.4 %copy.53 = f32[1,2,2,576,576]{4,3,2,1,0:T(8,128)} copy(f32[1,2,2,576,576]{3,4,1,2,0:T(8,128)} %bitcast_add_fusion) | data formatting | bytes 10616832
  181.7 1.0 maximum_bitcast_fusion
  182.7 16.4 %all_gather.52 = f32[2,2304,32]{2,0,1:T(2,128)S(1)} all-gather(f32[2,576,32]{2,0,1:T(2,128)S(1)} %copy-done.4), channel_id=1, replica_groups=mesh['dom'=2,'row'=4,'col'=4] {'row'}, dimensions={1}, use_global_device_ids=true | all-gather | bytes 737280 | tf_op jit(solution)/shard_map/all_gather | solution.py:82
  199.2 1.0 pad_maximum_fusion
  200.3 18.3 %convolution_bitcast_fusion = f32[1152,1152]{0,1:T(8,128)} fusion(f32[768,1152]{1,0:T(8,128)} %all-gather.8.cloned.1.call-done, f32[1152,768]{0,1:T(8,128)} %all-gather.10.cloned.1.call-done), kind=kOutput, calls=%fused_computation.1 | convolution fusion | flops 12230590464 | bytes 12386304 | tf_op jit(solution)/shard_map/dot_general | solution.py:10
  218.6 8.2 %reshape.155 = f32[2,576,2,576]{1,0,3,2:T(2,128)} reshape(f32[1152,1152]{0,1:T(8,128)} %convolution_bitcast_fusion) | data formatting | bytes 10616832 | tf_op jit(solution)/shard_map/reshape | solution.py:73
  226.8 9.1 %copy.46 = f32[2,576,2,576]{3,1,2,0:T(8,128)} copy(f32[2,576,2,576]{1,0,3,2:T(2,128)} %reshape.155) | data formatting | bytes 10616832 | tf_op jit(solution)/shard_map/reshape | solution.py:73
  235.9 20.5 %all-gather.12.cloned.1.call-done = f32[192,4608]{1,0:T(8,128)} async-done(((f32[192,1152]{1,0:T(8,128)}), f32[192,4608]{1,0:T(8,128)}) %all-gather.12.cloned.1.call-update) | async-done | bytes 3538960 | tf_op jit(solution)/shard_map/all_gather | solution.py:14
  256.3 6.4 %reshape.156 = f32[192,4,2,576]{3,2,1,0:T(2,128)} reshape(f32[192,4608]{1,0:T(8,128)} %all-gather.12.cloned.1.call-done) | data formatting | bytes 7077888 | tf_op jit(solution)/shard_map/reshape | solution.py:77
  262.8 5.1 %copy.48 = f32[192,2,4,576]{3,2,0,1:T(4,128)} copy(f32[192,2,4,576]{3,1,2,0:T(2,128)} %bitcast.78) | data formatting | bytes 7077888 | tf_op jit(solution)/shard_map/transpose | solution.py:77
  267.8 5.4 %reshape.157 = f32[192,2,2304]{2,0,1:T(8,128)} reshape(f32[192,2,4,576]{3,2,0,1:T(4,128)} %copy.48) | data formatting | bytes 7077888 | tf_op jit(solution)/shard_map/reshape | solution.py:78
  273.3 6.6 %fusion.2 = f32[192,32]{0,1:T(8,128)} fusion(f32[192,2,2304]{2,0,1:T(8,128)} %reshape.157, f32[2,2304,32]{2,0,1:T(2,128)S(1)} %all_gather.52), kind=kOutput, calls=%fused_computation.12 | convolution fusion | flops 339738624 | bytes 4153344 | tf_op jit(solution)/shard_map/pcn,cnq->pq/dot_general | solution.py:79
  279.9 6.0 %bitcast_add_fusion.1 = f32[2,2,576,576]{3,2,1,0:T(8,128)} fusion(f32[2,576,2,576]{3,1,2,0:T(8,128)} %copy.46, f32[2,576,576]{2,1,0:T(8,128)S(1)} %copy-done.3, f32[2,2]{1,0:T(2,128)S(1)} %copy.47), kind=kLoop, calls=%fused_computation.3 | loop fusion | flops 2654208 | bytes 13271056 | tf_op jit(solution)/shard_map/add | solution.py:75
  (53 shorter events, 6.5 us)
Async XLA Ops:
  7.2 158.5 %copy-start = (f32[1,2,576,192]{2,3,1,0:T(8,128)S(1)}, f32[1,2,576,192]{2,3,1,0:T(8,128)}, u32[]{:S(2)}) copy-start(f32[1,2,576,192]{2,3,1,0:T(8,128)} %param.15) | copy-start | bytes 2654212
  7.2 2.6 copy-start.5
  7.2 142.5 %all-gather.6.cloned.1.call-start = ((), (), s32[]{:S(2)}) async-start(), calls=%async_computation | async-start | bytes 4423680 | tf_op jit(solution)/shard_map/all_gather | solution.py:18
  8.6 3.7 %copy-start.7 = (f32[2,192,192]{2,1,0:T(8,128)S(1)}, f32[2,192,192]{2,1,0:T(8,128)}, u32[]{:S(2)}) copy-start(f32[2,192,192]{2,1,0:T(8,128)} %param.12) | copy-start | bytes 884740
  9.8 190.5 %all-gather.10.cloned.1.call-start = ((), (), s32[]{:S(2)}) async-start(), calls=%async_computation.2 | async-start | bytes 4423680 | tf_op jit(solution)/shard_map/all_gather | solution.py:14
  12.2 188.1 %all-gather.8.cloned.1.call-start = ((), (), s32[]{:S(2)}) async-start(), calls=%async_computation.1 | async-start | bytes 4423680 | tf_op jit(solution)/shard_map/all_gather | solution.py:18
  149.7 6.3 %copy-start.9 = (f32[2,576,32]{1,2,0:T(8,128)S(1)}, f32[2,576,32]{1,2,0:T(8,128)}, u32[]{:S(2)}) copy-start(f32[2,576,32]{1,2,0:T(8,128)} %param.13) | copy-start | bytes 442372
  155.3 101.0 %all-gather.12.cloned.1.call-start = ((), (), s32[]{:S(2)}) async-start(), calls=%async_computation.3 | async-start | bytes 4423680 | tf_op jit(solution)/shard_map/all_gather | solution.py:14
  155.9 4.6 %copy-start.8 = (f32[1,2,192,192]{3,2,1,0:T(8,128)S(1)}, f32[1,2,192,192]{3,2,1,0:T(8,128)}, u32[]{:S(2)}) copy-start(f32[1,2,192,192]{3,2,1,0:T(8,128)} %param.17) | copy-start | bytes 884740
  160.5 3.3 %copy-start.6 = (f32[1,2,192,576]{3,2,1,0:T(8,128)S(1)}, f32[1,2,192,576]{3,2,1,0:T(8,128)}, u32[]{:S(2)}) copy-start(f32[1,2,192,576]{3,2,1,0:T(8,128)} %param.16) | copy-start | bytes 2654212
  181.5 1.2 copy-start.4
  181.5 17.6 %copy-start.2 = (f32[192,1152]{1,0:T(8,128)S(1)}, f32[192,1152]{1,0:T(8,128)}, u32[]{:S(2)}) copy-start(f32[192,1152]{1,0:T(8,128)} %convolution_negate_fusion.1) | copy-start | bytes 2654212
  273.3 6.6 %copy-start.3 = (f32[2,576,576]{2,1,0:T(8,128)S(1)}, f32[2,576,576]{2,1,0:T(8,128)}, u32[]{:S(2)}) copy-start(f32[2,576,576]{2,1,0:T(8,128)} %param.9) | copy-start | bytes 7962628
  279.9 6.0 %copy-start.1 = (f32[1,2,576,192]{2,3,1,0:T(8,128)S(1)}, f32[1,2,576,192]{2,3,1,0:T(8,128)}, u32[]{:S(2)}) copy-start(f32[1,2,576,192]{2,3,1,0:T(8,128)} %param.15) | copy-start | bytes 2654212
Sparse Core Ops, SparseCore 0:
  10.2 37.5 all-gather.5
  49.3 85.3 all-gather.9
  155.4 29.2 all-gather.7
  186.2 70.1 all-gather.11
where the time goes:
time: 293 us; the launch traced here: 292 us
  blocking collectives  149 us (51%)
  local copies, waits for them, and re-layouts  53 us (18%)
  matrix products  46.4 us (16%)
  waiting for transfers between devices  20.8 us (7%)
  between operations  14 us (5%)
  other arithmetic  9.26 us (3%)
    all_gather x4, blocking collectives, panel(): return lax.all_gather(block, 'col', axis=1, tiled=True)  94.4 us
    dot_general x12, matrix products, matmul(): jnp.dot(a, b, precision=lax.Precision.HIGHEST, preferred_element_type=jnp...  39.8 us
    all_gather x4, blocking collectives, fold_product(): lax.all_gather(right_block, 'row', axis=0, tiled=True)  37.8 us
    all_gather x2, waiting for transfers between devices, panel(): return lax.all_gather(block, 'col', axis=1, tiled=True)  20.5 us
    reshape x2, local copies, waits for them, and re-layouts, shards(): lifted = lifted.reshape(2, ext_rows, 2, third).transpose(0, 2, 1, 3)  17.3 us
    all_gather x1, blocking collectives, shards(): lax.all_gather(boundary_data, 'row', axis=1, tiled=True)  16.4 us
    unnamed x23, local copies, waits for them, and re-layouts  8.23 us
    dot_general x1, matrix products, shards(): jnp.einsum('pcn,cnq->pq', operator_rows, lax.all_gather(boundary_data, 'r...  6.59 us
  transfers between devices with their start and end apart: 4, of which 1 were waited for; matrix products, arithmetic and copies ran while one was open for 26% of the time, Pallas kernels for 0%

commit v1 on v0

--- a/solution.py
+++ b/solution.py
@@ -1,9 +1,488 @@
+import functools
+
 import jax
 import jax.numpy as jnp
 from jax import lax
+from jax.experimental import pallas as pl
+from jax.experimental.pallas import tpu as pltpu
 from jax.sharding import PartitionSpec as P
 
+MESH = pl.DeviceIdType.MESH
+BF = jnp.bfloat16
+F32 = jnp.float32
 ITERS = 2
+
+
+def split(x):
+    hi = x.astype(BF)
+    return hi, (x - hi.astype(F32)).astype(BF)
+
+
+def dot(a, b):
+    return jnp.dot(a, b, preferred_element_type=F32)
+
+
+def dot3(ah, al, bh, bl):
+    return dot(ah, bh) + (dot(ah, bl) + dot(al, bh))
+
+
+def first_step(joint):
+    n = joint.shape[0]
+    eye = lax.broadcasted_iota(jnp.int32, (n, n), 0) == lax.broadcasted_iota(jnp.int32, (n, n), 1)
+    kept = jnp.where(eye, joint, 0.0)
+    down = 1.0 / jnp.sum(kept, axis=1, keepdims=True)
+    across = 1.0 / jnp.sum(kept, axis=0, keepdims=True)
+    return jnp.where(eye, 2.0 * across, 0.0) - down * joint * across
+
+
+def up128(n):
+    return -(-n // 128) * 128
+
+
+def kernel(
+    R, C, M, PK,
+    ee, ei, ie, ii, bd, lee, lei, lie, lii,
+    parent, solve, iv, lparent, lsolve,
+    eg, cg, jg, bdp, bdr, ivs, ivr,
+    ein, cin, jin, bdin, eev, leev, leiv, liev, liiv,
+    pv, sv, ivv, lpv, lsv,
+    big, jh, jl, xh, xl, wh, wl, ch, cl, sh, sl,
+    lch, lcl, lsh, lsl, ah, al,
+    load, e_recv, e_up, e_dn, jz_send, jz_recv, jp_send, jp_recv, cp_send, cp_recv,
+    b_sem, iv_send, iv_recv, out_sem, lp_sem, pm_sem,
+):
+    d, r, z = lax.axis_index("dom"), lax.axis_index("row"), lax.axis_index("col")
+    mate = r + 1 - 2 * lax.rem(r, 2)
+    core = lax.rem(r, 2)
+    chip = lax.div(r, 2)
+    X = R // 2
+    h, w = ii.shape[1], ii.shape[2]
+    t, u = ei.shape[1], ei.shape[2]
+    T = up128(t)
+    n = R * h
+    tm = t // M
+    src_cols = bd.shape[2]
+
+    loads = [
+        pltpu.make_async_copy(s, v, load.at[k])
+        for k, (s, v) in enumerate(
+            [(ii, jin), (ei, ein), (ie, cin), (bd, bdin), (lii, liiv), (lie, liev), (lei, leiv), (lee, leev), (ee, eev)]
+        )
+    ]
+    for c in loads:
+        c.start()
+
+    barrier = pltpu.get_barrier_semaphore()
+
+    @pl.loop(0, R)
+    def _(a):
+        @pl.loop(0, C)
+        def _(b):
+            @pl.when(jnp.logical_or(a != r, b != z))
+            def _():
+                pl.semaphore_signal(barrier, inc=1, device_id={"row": a, "col": b}, device_id_type=MESH)
+
+    loads[0].wait()
+    half = h // 2
+    own_j = jin[0] + jin[1]
+    jg[r, z, :, :w] = own_j[:half]
+    jg[r, z, :, w:] = own_j[half:]
+    loads[1].wait()
+    eg[z, :, :u] = ein[0]
+    eg[z, :, u:] = ein[1]
+    loads[2].wait()
+    here = pl.multiple_of(r * h, h)
+    cg[pl.ds(here, h), :t] = cin[0]
+    cg[pl.ds(here, h), t:] = cin[1]
+    loads[3].wait()
+    part = t // (PK // 2)
+    for q in range(PK):
+        a, o = q // (PK // 2), (q % (PK // 2)) * part
+        bdp[:, q * src_cols:(q + 1) * src_cols] = bdin[a, o:o + part]
+
+    pl.semaphore_wait(barrier, R * C - 1)
+
+    def jz(to):
+        return pltpu.make_async_remote_copy(
+            jg.at[r, z], jg.at[r, z], jz_send.at[to], jz_recv.at[z], device_id={"col": to}, device_id_type=MESH)
+
+    def jz_in(frm):
+        return pltpu.make_async_remote_copy(
+            jg.at[r, frm], jg.at[r, frm], jz_send.at[frm], jz_recv.at[frm], device_id={"col": frm}, device_id_type=MESH)
+
+    @pl.loop(0, C)
+    def _(b):
+        @pl.when(b != z)
+        def _():
+            jz(b).start()
+
+    def e_copy(src, m, up):
+        rows = pl.ds(pl.multiple_of(m * tm, 8), tm)
+        to = z + 1 if up else z - 1
+        return pltpu.make_async_remote_copy(
+            eg.at[src, rows], eg.at[src, rows], (e_up if up else e_dn).at[src, m], e_recv.at[src, m],
+            device_id={"col": to}, device_id_type=MESH)
+
+    can_up, can_dn = z < C - 1, z > 0
+
+    @pl.loop(0, M)
+    def _(m):
+        @pl.when(can_up)
+        def _():
+            e_copy(z, m, True).start()
+
+        @pl.when(can_dn)
+        def _():
+            e_copy(z, m, False).start()
+
+    def forward(s, lo, hi):
+        @pl.loop(lo, hi)
+        def _(m):
+            @pl.when(jnp.logical_and(can_up, z >= s))
+            def _():
+                e_copy(z - s, m, True).wait_recv()
+                e_copy(z - s, m, True).start()
+
+            @pl.when(jnp.logical_and(can_dn, z + s <= C - 1))
+            def _():
+                e_copy(z + s, m, False).wait_recv()
+                e_copy(z + s, m, False).start()
+
+    def c_copy(row, to, k):
+        rows = pl.ds(pl.multiple_of(row * h, h), h)
+        return pltpu.make_async_remote_copy(
+            cg.at[rows], cg.at[rows], cp_send.at[k], cp_recv.at[row], device_id={"row": to}, device_id_type=MESH)
+
+    def j_copy(row, to, k):
+        return pltpu.make_async_remote_copy(
+            jg.at[row], jg.at[row], jp_send.at[k], jp_recv.at[row], device_id={"row": to}, device_id_type=MESH)
+
+    def spread_own(copy):
+        @pl.loop(0, X)
+        def _(x):
+            @pl.when(x != chip)
+            def _():
+                copy(r, 2 * x + core, x).start()
+
+        copy(r, mate, chip).start()
+
+    def relay(copy):
+        @pl.loop(0, X)
+        def _(x):
+            @pl.when(x != chip)
+            def _():
+                copy(2 * x + core, mate, X + x).wait_recv()
+                copy(2 * x + core, mate, X + x).start()
+
+    def settle(copy):
+        copy(mate, mate, chip).wait_recv()
+
+        @pl.loop(0, X)
+        def _(x):
+            @pl.when(x != chip)
+            def _():
+                copy(2 * x + 1 - core, mate, X + x).wait_recv()
+
+    def finish(copy):
+        copy(r, mate, chip).wait_send()
+
+        @pl.loop(0, X)
+        def _(x):
+            @pl.when(x != chip)
+            def _():
+                copy(r, 2 * x + core, x).wait_send()
+                copy(2 * x + core, mate, X + x).wait_send()
+
+    spread_own(c_copy)
+
+    crossed = pltpu.make_async_remote_copy(
+        bdp, bdr, b_sem.at[0], b_sem.at[1], device_id={"row": z, "col": r}, device_id_type=MESH)
+
+    @pl.when(r != z)
+    def _():
+        crossed.start()
+
+    @pl.when(r == z)
+    def _():
+        bdr[...] = bdp[...]
+
+    loads[4].wait()
+    loads[5].wait()
+    lj = liiv[0] + liiv[1]
+    x1 = first_step(lj)
+    x1h, x1l = split(x1)
+    ljh, ljl = split(lj)
+    lw = dot3(ljh, ljl, x1h, x1l)
+    x2 = dot3(x1h, x1l, *split(lw)) - 2.0 * x1
+    x2h, x2l = split(x2)
+    nl = lj.shape[0]
+    tl = lie.shape[2]
+    TL = up128(tl)
+    for b in range(2):
+        lch[:, b * TL:b * TL + tl], lcl[:, b * TL:b * TL + tl] = split(liev[b])
+        got = dot3(x2h, x2l, lch[:, b * TL:b * TL + tl], lcl[:, b * TL:b * TL + tl])
+        lsv[b] = got
+        lsh[:, b * TL:b * TL + tl], lsl[:, b * TL:b * TL + tl] = split(got)
+    ls_out = pltpu.make_async_copy(lsv, lsolve, out_sem.at[0])
+    ls_out.start()
+
+    @pl.loop(0, C)
+    def _(b):
+        @pl.when(b != z)
+        def _():
+            jz_in(b).wait_recv()
+
+    spread_own(j_copy)
+
+    loads[6].wait()
+    loads[7].wait()
+    for a in range(2):
+        @pl.loop(0, tl // nl)
+        def _(m):
+            rows = pl.ds(pl.multiple_of(m * nl, nl), nl)
+            eh, el = split(leiv[a, rows])
+            for b in range(2):
+                cols = slice(b * TL, b * TL + tl)
+                got = dot3(eh, el, lsh[:, cols], lsl[:, cols])
+                lpv[a, b, rows] = got + leev[a, rows] if a == b else got
+                pltpu.make_async_copy(lpv.at[a, b, rows], lparent.at[a, b, rows], lp_sem.at[2 * a + b, m]).start()
+
+    mh = M // 2
+    forward(1, 0, mh)
+    relay(c_copy)
+    settle(c_copy)
+    for b in range(2):
+        @pl.loop(0, R)
+        def _(k):
+            rows = pl.ds(pl.multiple_of(k * h, h), h)
+            ch[rows, b * T:b * T + t], cl[rows, b * T:b * T + t] = split(cg[rows, b * t:(b + 1) * t])
+    forward(1, mh, M)
+    relay(j_copy)
+    settle(j_copy)
+    for a in range(R):
+        for b in range(C):
+            big[a * h:a * h + half, b * w:(b + 1) * w] = jg[a, b, :, :w]
+            big[a * h + half:(a + 1) * h, b * w:(b + 1) * w] = jg[a, b, :, w:]
+    joint = big[...]
+    jh[...], jl[...] = split(joint)
+    x1 = first_step(joint)
+    big[...] = x1
+    xh[...], xl[...] = split(x1)
+
+    @pl.loop(0, R)
+    def _(k):
+        rows = pl.ds(pl.multiple_of(k * h, h), h)
+        wh[rows], wl[rows] = split(dot3(jh[rows], jl[rows], xh[...], xl[...]))
+
+    for s in range(2, C - 1):
+        forward(s, 0, mh)
+
+    @pl.loop(0, R)
+    def _(k):
+        rows = pl.ds(pl.multiple_of(k * h, h), h)
+        jh[rows], jl[rows] = split(dot3(xh[rows], xl[rows], wh[...], wl[...]) - 2.0 * big[rows])
+
+    for s in range(2, C - 1):
+        forward(s, mh, M)
+
+    @pl.loop(0, R)
+    def _(k):
+        rows = pl.ds(pl.multiple_of(k * h, h), h)
+        for b in range(2):
+            cols = slice(b * T, b * T + t)
+            got = dot3(jh[rows], jl[rows], ch[:, cols], cl[:, cols])
+            sh[rows, cols], sl[rows, cols] = split(got)
+
+            @pl.when(k == r)
+            def _():
+                sv[b] = got
+
+    s_out = pltpu.make_async_copy(sv, solve, out_sem.at[1])
+    s_out.start()
+
+    @pl.when(r != z)
+    def _():
+        crossed.wait_recv()
+
+    flat = jnp.concatenate([bdr[:, q * src_cols:(q + 1) * src_cols] for q in range(PK)], axis=0)
+    fh, fl = split(flat)
+    quarter = h // PK
+    for k in range(R):
+        rows = slice(k * h, (k + 1) * h)
+        got = dot3(sh[rows, :t], sl[rows, :t], fh[:t], fl[:t])
+        got += dot3(sh[rows, T:T + t], sl[rows, T:T + t], fh[t:], fl[t:])
+        for q in range(PK):
+            ivs[k, :, q * src_cols:(q + 1) * src_cols] = got[q * quarter:(q + 1) * quarter]
+
+    def iv_copy(k):
+        return pltpu.make_async_remote_copy(
+            ivs.at[k], ivr.at[z], iv_send.at[k], iv_recv.at[z], device_id={"row": k, "col": r}, device_id_type=MESH)
+
+    def iv_in(c):
+        return pltpu.make_async_remote_copy(
+            ivs.at[r], ivr.at[c], iv_send.at[c], iv_recv.at[c], device_id={"row": z, "col": c}, device_id_type=MESH)
+
+    for k in range(R):
+        own = jnp.logical_and(r == k, r == z)
+
+        @pl.when(jnp.logical_not(own))
+        def _():
+            iv_copy(k).start()
+
+        @pl.when(own)
+        def _():
+            ivr[z] = ivs[k]
+
+    loads[8].wait()
+
+    @pl.loop(0, M)
+    def _(m):
+        @pl.when(z == C - 1)
+        def _():
+            @pl.loop(0, C - 1)
+            def _(i):
+                s = C - 2 - i
+                e_copy(s, m, False).wait_recv()
+
+        @pl.when(z == 0)
+        def _():
+            @pl.loop(1, C)
+            def _(s):
+                e_copy(s, m, True).wait_recv()
+
+        rows = pl.ds(pl.multiple_of(m * tm, 8), tm)
+        for c in range(C):
+            for a in range(2):
+                o = slice(a * tm, (a + 1) * tm)
+                ah[o, c * u:(c + 1) * u], al[o, c * u:(c + 1) * u] = split(eg[c, rows, a * u:(a + 1) * u])
+        for b in range(2):
+            cols = slice(b * T, b * T + t)
+            got = dot3(ah[...], al[...], sh[:, cols], sl[:, cols])
+            for a in range(2):
+                one = got[a * tm:(a + 1) * tm]
+                pv[a, b, rows] = one + eev[a, rows] if a == b else one
+                pltpu.make_async_copy(pv.at[a, b, rows], parent.at[a, b, rows], pm_sem.at[2 * a + b, m]).start()
+
+    @pl.loop(0, C)
+    def _(c):
+        @pl.when(jnp.logical_not(jnp.logical_and(r == z, c == z)))
+        def _():
+            iv_in(c).wait_recv()
+
+    total = ivr[0]
+    for c in range(1, C):
+        total = total + ivr[c]
+    for q in range(PK):
+        ivv[q * quarter:(q + 1) * quarter] = total[:, q * src_cols:(q + 1) * src_cols]
+    iv_out = pltpu.make_async_copy(ivv, iv, out_sem.at[2])
+    iv_out.start()
+
+    @pl.loop(0, C)
+    def _(b):
+        @pl.when(b != z)
+        def _():
+            jz(b).wait_send()
+
+    finish(c_copy)
+    finish(j_copy)
+
+    @pl.when(r != z)
+    def _():
+        crossed.wait_send()
+
+    for k in range(R):
+        @pl.when(jnp.logical_not(jnp.logical_and(r == k, r == z)))
+        def _():
+            iv_copy(k).wait_send()
+
+    @pl.loop(0, M)
+    def _(m):
+        @pl.when(can_up)
+        def _():
+            @pl.loop(0, z + 1)
+            def _(s):
+                e_copy(s, m, True).wait_send()
+
+        @pl.when(can_dn)
+        def _():
+            @pl.loop(z, C)
+            def _(s):
+                e_copy(s, m, False).wait_send()
+
+        rows = pl.ds(pl.multiple_of(m * tm, 8), tm)
+        for a in range(2):
+            for b in range(2):
+                pltpu.make_async_copy(pv.at[a, b, rows], parent.at[a, b, rows], pm_sem.at[2 * a + b, m]).wait()
+
+    @pl.loop(0, tl // nl)
+    def _(m):
+        rows = pl.ds(pl.multiple_of(m * nl, nl), nl)
+        for a in range(2):
+            for b in range(2):
+                pltpu.make_async_copy(lpv.at[a, b, rows], lparent.at[a, b, rows], lp_sem.at[2 * a + b, m]).wait()
+
+    ls_out.wait()
+    s_out.wait()
+    iv_out.wait()
+
+
+def fused(R, C, ee, ei, ie, ii, bd, lee, lei, lie, lii):
+    lee, lei, lie, lii = lee[0], lei[0], lie[0], lii[0]
+    h, w = ii.shape[1:]
+    t, u = ei.shape[1:]
+    nl, tl = lie.shape[1:]
+    T, TL = up128(t), up128(tl)
+    n = R * h
+    q = bd.shape[2]
+    PK = 128 // q
+    M = 6
+    tm = t // M
+    V = pltpu.VMEM
+    D = pltpu.SemaphoreType.DMA
+    scratch = [
+        V((C, t, 2 * u), F32), V((n, 2 * t), F32), V((R, C, h // 2, 2 * w), F32),
+        V((2 * t // PK, 128), F32), V((2 * t // PK, 128), F32), V((R, h // PK, 128), F32), V((C, h // PK, 128), F32),
+        V(ei.shape, F32), V(ie.shape, F32), V(ii.shape, F32), V(bd.shape, F32), V(ee.shape, F32),
+        V(lee.shape, F32), V(lei.shape, F32), V(lie.shape, F32), V(lii.shape, F32),
+        V((2, 2, t, t), F32), V((2, h, t), F32), V((h, q), F32), V((2, 2, tl, tl), F32), V((2, nl, tl), F32),
+        V((n, n), F32), V((n, n), BF), V((n, n), BF), V((n, n), BF), V((n, n), BF), V((n, n), BF), V((n, n), BF),
+        V((n, 2 * T), BF), V((n, 2 * T), BF), V((n, 2 * T), BF), V((n, 2 * T), BF),
+        V((nl, 2 * TL), BF), V((nl, 2 * TL), BF), V((nl, 2 * TL), BF), V((nl, 2 * TL), BF),
+        V((2 * tm, n), BF), V((2 * tm, n), BF),
+        D((9,)), D((C, M)), D((C, M)), D((C, M)), D((C,)), D((C,)), D((R,)), D((R,)), D((R,)), D((R,)),
+        D((2,)), D((R,)), D((C,)), D((3,)), D((4, tl // nl)), D((4, M)),
+    ]
+    outs = (
+        jax.ShapeDtypeStruct((2, 2, t, t), F32),
+        jax.ShapeDtypeStruct((2, h, t), F32),
+        jax.ShapeDtypeStruct((h, q), F32),
+        jax.ShapeDtypeStruct((2, 2, tl, tl), F32),
+        jax.ShapeDtypeStruct((2, nl, tl), F32),
+    )
+    got = pl.pallas_call(
+        functools.partial(kernel, R, C, M, PK),
+        out_shape=outs,
+        in_specs=[pl.BlockSpec(memory_space=pl.ANY)] * 9,
+        out_specs=[pl.BlockSpec(memory_space=pl.ANY)] * 5,
+        scratch_shapes=scratch,
+        compiler_params=pltpu.CompilerParams(
+            collective_id=0, has_side_effects=True, vmem_limit_bytes=60 * 1024 * 1024),
+        cost_estimate=pl.CostEstimate(flops=18 * n * n * t * 4, bytes_accessed=24 * t * t * 4, transcendentals=0),
+    )(ee, ei, ie, ii, bd, lee, lei, lie, lii)
+    return got[0], got[1], got[2], got[3][None], got[4][None]
+
+
+def fits(R, C, shapes):
+    h, w = shapes[3][1] // R, shapes[3][2] // C
+    t, u = shapes[1][1] // R, shapes[1][2] // C
+    q = shapes[4][2] // C
+    nl, tl = shapes[7][2:]
+    boxes = shapes[5][0]
+    return (
+        R == C and R % 2 == 0 and C >= 3 and h == w == u and h % 16 == 0 and (2 * u) % 128 == 0 and t % 48 == 0
+        and 128 % q == 0 and h % (8 * (128 // q)) == 0 and (2 * t) % (8 * (128 // q)) == 0
+        and (128 // q) % 2 == 0 and tl % nl == 0 and nl % 16 == 0
+    )
 
 
 def matmul(a, b):
@@ -104,4 +583,13 @@
         P(("dom", "row", "col"), None, None, None, None),
         P(("dom", "row", "col"), None, None, None),
     )
-    return jax.shard_map(shards, mesh=mesh, in_specs=in_specs, out_specs=out_specs, check_vma=False)
+
+    def run(*args):
+        shapes = [a.shape for a in args]
+        R, C = mesh.shape["row"], mesh.shape["col"]
+        one_box = shapes[5][0] == mesh.shape["dom"] * R * C
+        two_maps = shapes[0][0] == 2 * mesh.shape["dom"]
+        body = functools.partial(fused, R, C) if one_box and two_maps and fits(R, C, shapes) else shards
+        return jax.shard_map(body, mesh=mesh, in_specs=in_specs, out_specs=out_specs, check_vma=False)(*args)
+
+    return run

time: 293 us -> 105 us (0.36)
  blocking collectives: 149 us -> 0 us
  Pallas kernels: 0 us -> 84.6 us
  matrix products: 46.4 us -> 0 us
  local copies, waits for them, and re-layouts: 53 us -> 19.1 us
  waiting for transfers between devices: 20.8 us -> 0 us
  between operations: 14 us -> 0.66 us
  other arithmetic: 9.26 us -> 0.01 us
    all_gather x9 -> x0, blocking collectives: 149 us -> none  [the longest x4 94.4 us: panel(): return lax.all_gather(block, 'col', axis=1, tiled=True)]
    pallas_call x0 -> x1, Pallas kernels: none -> 84.6 us  [fused(): pl.pallas_call(functools.partial(kernel, R, C, M, PK), out_shape=outs, in...]
    dot_general x13 -> x0, matrix products: 46.4 us -> none  [the longest x12 39.8 us: matmul(): jnp.dot(a, b, precision=lax.Precision.HIGHEST, preferred_element_type=jnp...]
    reshape x5 -> x0, local copies, waits for them, and re-layouts: 30.8 us -> none  [the longest x2 17.3 us: shards(): lifted = lifted.reshape(2, ext_rows, 2, third).transpose(0, 2, 1, 3)]
    all_gather x4 -> x0, waiting for transfers between devices: 20.5 us -> none  [the longest x2 20.5 us: panel(): return lax.all_gather(block, 'col', axis=1, tiled=True)]
    unnamed x23 -> x16, local copies, waits for them, and re-layouts: 8.23 us -> 19.1 us
    add x3 -> x0, other arithmetic: 6.01 us -> none  [the longest x1 5.98 us: shards(): parent_map = lifted + pairs[:, :, None, None] * ext_ext[:, None]]
    transpose x1 -> x0, local copies, waits for them, and re-layouts: 5.08 us -> none  [shards(): operator_rows.reshape(rows_here, n_col, 2, third).transpose(0, 2, 1, 3)]
  transfers between devices with their start and end apart: 4 -> 0, of which waited for: 1 -> 0; matrix products, arithmetic and copies ran while one was open for 26% -> 0% of each run, Pallas kernels for 0% -> 0%
where the time goes in v1:
time: 105 us; the launch traced here: 104 us
  Pallas kernels  84.6 us (81%)
  local copies, waits for them, and re-layouts  19.1 us (18%)
    pallas_call x1, Pallas kernels, fused(): pl.pallas_call(functools.partial(kernel, R, C, M, PK), out_shape=outs, in...  84.6 us
    unnamed x16, local copies, waits for them, and re-layouts  19.1 us

profile of v1, /device:TPU:0, one launch (start us, length us, event | category | flops | bytes accessed | tf_op | source)
XLA Modules:
  0.0 104.4 jit_solution(1413953170589918043)
XLA Ops:
  0.6 2.0 %copy.16.bd = f32[2,576,32]{2,1,0:T(8,128)} copy(f32[2,576,32]{1,2,0:T(8,128)} %param.13) | data formatting | bytes 294912 | tf_op args[4]
  2.6 2.6 %copy.15.ei = f32[2,576,192]{2,1,0:T(8,128)} copy(f32[2,576,192]{1,2,0:T(8,128)} %param.10) | data formatting | bytes 1769472 | tf_op args[1]
  5.2 2.6 %copy.14 = f32[1,2,576,192]{3,2,1,0:T(8,128)} copy(f32[1,2,576,192]{2,3,1,0:T(8,128)} %param.15) | data formatting | bytes 1769472 | tf_op args[6]
  7.8 84.6 %shard_map.128 = (f32[2,2,576,576]{3,2,1,0:T(8,128)}, f32[2,192,576]{2,1,0:T(8,128)}, f32[192,32]{1,0:T(8,128)}, f32[2,2,576,576]{3,2,1,0:T(8,128)}, f32[2,192,576]{2,1,0:T(8,128)}) custom-call(f32[2,576,576]{2,1,0:T(8,128)} %ee.1, f32[2,576,192]{2,1,0:T(8,128)} %copy.15.ei, f32[2,192,576]{2,1,0:T(8,128)} %ie.1, f32[2,192,192]{2,1,0:T(8,128)} %ii.1, ...), custom_call_target="tpu_custom_call" | custom-call | flops 24461180928 | bytes 31850496 | tf_op jit(solution)/shard_map/pallas_call | solution.py:462
  92.4 0.0 slice-start
  92.4 1.7 %copy.17 = f32[192,32]{0,1:T(8,128)} copy(f32[192,32]{1,0:T(8,128)} %get-tuple-element.17) | data formatting | bytes 49152
  94.1 0.0 copy-start.1
  94.1 0.0 slice-start.1
  94.1 5.8 %copy.22 = f32[2,2,576,576]{3,2,1,0:T(8,128)} copy(f32[2,2,576,576]{3,2,1,0:T(8,128)} %get-tuple-element.25) | data formatting | bytes 10616832
  99.9 0.0 copy-done.1
  99.9 0.9 copy.23
  100.9 0.0 slice-done
  100.9 0.0 slice-done.1
  100.9 0.0 copy-start
  100.9 2.6 %copy.24 = f32[1,2,2,576,576]{4,3,2,1,0:T(8,128)} copy(f32[1,2,2,576,576]{4,3,2,1,0:T(8,128)S(1)} %bitcast.8) | data formatting | bytes 10616832
  103.4 0.0 copy-done
  103.4 0.9 copy.25
  (1 shorter events, 0.0 us)
Async XLA Ops:
  92.4 8.5 %slice-start = ((s8[5898240]{0:T(1024)(128)(4,1)}), s8[1703936]{0:T(1024)(128)(4,1)S(1)}, s32[]{:S(2)}) async-start(s8[5898240]{0:T(1024)(128)(4,1)} %bitcast.6), calls=%async_computation | async-start | bytes 3407872
  94.1 5.8 %copy-start.1 = (f32[2,192,576]{2,1,0:T(8,128)S(1)}, f32[2,192,576]{2,1,0:T(8,128)}, u32[]{:S(2)}) copy-start(f32[2,192,576]{2,1,0:T(8,128)} %get-tuple-element.26) | copy-start | bytes 2654212
  94.1 6.7 %slice-start.1 = ((s8[5898240]{0:T(1024)(128)(4,1)}), s8[4194304]{0:T(1024)(128)(4,1)S(1)}, s32[]{:S(2)}) async-start(s8[5898240]{0:T(1024)(128)(4,1)} %bitcast.6), calls=%async_computation.1 | async-start | bytes 8388608
  100.9 2.6 %copy-start = (f32[2,192,576]{2,1,0:T(8,128)S(1)}, f32[2,192,576]{2,1,0:T(8,128)}, u32[]{:S(2)}) copy-start(f32[2,192,576]{2,1,0:T(8,128)} %get-tuple-element.14) | copy-start | bytes 2654212

commit v2 on v1

--- a/solution.py
+++ b/solution.py
@@ -24,6 +24,14 @@
 
 def dot3(ah, al, bh, bl):
     return dot(ah, bh) + (dot(ah, bl) + dot(al, bh))
+
+
+def dot_t(a, b):
+    return lax.dot_general(a, b, (((1,), (1,)), ((), ())), preferred_element_type=F32)
+
+
+def dot3t(ah, al, bh, bl):
+    return dot_t(ah, bh) + (dot_t(ah, bl) + dot_t(al, bh))
 
 
 def first_step(joint):
@@ -40,11 +48,11 @@
 
 
 def kernel(
-    R, C, M, PK,
+    R, C, M,
     ee, ei, ie, ii, bd, lee, lei, lie, lii,
     parent, solve, iv, lparent, lsolve,
     eg, cg, jg, bdp, bdr, ivs, ivr,
-    ein, cin, jin, bdin, eev, leev, leiv, liev, liiv,
+    ein, cin, jin, eev, leev, leiv, let, liev, liiv,
     pv, sv, ivv, lpv, lsv,
     big, jh, jl, xh, xl, wh, wl, ch, cl, sh, sl,
     lch, lcl, lsh, lsl, ah, al,
@@ -57,16 +65,15 @@
     chip = lax.div(r, 2)
     X = R // 2
     h, w = ii.shape[1], ii.shape[2]
-    t, u = ei.shape[1], ei.shape[2]
+    t, u = ei.shape[2], ei.shape[1]
     T = up128(t)
     n = R * h
     tm = t // M
-    src_cols = bd.shape[2]
 
     loads = [
         pltpu.make_async_copy(s, v, load.at[k])
         for k, (s, v) in enumerate(
-            [(ii, jin), (ei, ein), (ie, cin), (bd, bdin), (lii, liiv), (lie, liev), (lei, leiv), (lee, leev), (ee, eev)]
+            [(ii, jin), (ei, ein), (ie, cin), (bd, bdp), (lii, liiv), (lie, liev), (lei, leiv), (lee, leev), (ee, eev)]
         )
     ]
     for c in loads:
@@ -88,17 +95,13 @@
     jg[r, z, :, :w] = own_j[:half]
     jg[r, z, :, w:] = own_j[half:]
     loads[1].wait()
-    eg[z, :, :u] = ein[0]
-    eg[z, :, u:] = ein[1]
+    eg[z, :, :u] = ein[0].T
+    eg[z, :, u:] = ein[1].T
     loads[2].wait()
     here = pl.multiple_of(r * h, h)
     cg[pl.ds(here, h), :t] = cin[0]
     cg[pl.ds(here, h), t:] = cin[1]
     loads[3].wait()
-    part = t // (PK // 2)
-    for q in range(PK):
-        a, o = q // (PK // 2), (q % (PK // 2)) * part
-        bdp[:, q * src_cols:(q + 1) * src_cols] = bdin[a, o:o + part]
 
     pl.semaphore_wait(barrier, R * C - 1)
 
@@ -237,10 +240,12 @@
     loads[6].wait()
     loads[7].wait()
     for a in range(2):
+        let[...] = leiv[a].T
+
         @pl.loop(0, tl // nl)
         def _(m):
             rows = pl.ds(pl.multiple_of(m * nl, nl), nl)
-            eh, el = split(leiv[a, rows])
+            eh, el = split(let[rows])
             for b in range(2):
                 cols = slice(b * TL, b * TL + tl)
                 got = dot3(eh, el, lsh[:, cols], lsl[:, cols])
@@ -304,15 +309,11 @@
     def _():
         crossed.wait_recv()
 
-    flat = jnp.concatenate([bdr[:, q * src_cols:(q + 1) * src_cols] for q in range(PK)], axis=0)
-    fh, fl = split(flat)
-    quarter = h // PK
+    fh, fl = split(bdr[...])
     for k in range(R):
         rows = slice(k * h, (k + 1) * h)
-        got = dot3(sh[rows, :t], sl[rows, :t], fh[:t], fl[:t])
-        got += dot3(sh[rows, T:T + t], sl[rows, T:T + t], fh[t:], fl[t:])
-        for q in range(PK):
-            ivs[k, :, q * src_cols:(q + 1) * src_cols] = got[q * quarter:(q + 1) * quarter]
+        got = dot3t(fh[0], fl[0], sh[rows, :t], sl[rows, :t])
+        ivs[k] = got + dot3t(fh[1], fl[1], sh[rows, T:T + t], sl[rows, T:T + t])
 
     def iv_copy(k):
         return pltpu.make_async_remote_copy(
@@ -372,8 +373,7 @@
     total = ivr[0]
     for c in range(1, C):
         total = total + ivr[c]
-    for q in range(PK):
-        ivv[q * quarter:(q + 1) * quarter] = total[:, q * src_cols:(q + 1) * src_cols]
+    ivv[...] = total
     iv_out = pltpu.make_async_copy(ivv, iv, out_sem.at[2])
     iv_out.start()
 
@@ -427,24 +427,24 @@
 
 
 def fused(R, C, ee, ei, ie, ii, bd, lee, lei, lie, lii):
-    lee, lei, lie, lii = lee[0], lei[0], lie[0], lii[0]
+    lee, lei, lie, lii = lee[0], jnp.swapaxes(lei[0], 1, 2), lie[0], lii[0]
+    ei, bd = jnp.swapaxes(ei, 1, 2), jnp.swapaxes(bd, 1, 2)
     h, w = ii.shape[1:]
-    t, u = ei.shape[1:]
+    u, t = ei.shape[1:]
     nl, tl = lie.shape[1:]
     T, TL = up128(t), up128(tl)
     n = R * h
-    q = bd.shape[2]
-    PK = 128 // q
+    q = bd.shape[1]
     M = 6
     tm = t // M
     V = pltpu.VMEM
     D = pltpu.SemaphoreType.DMA
     scratch = [
         V((C, t, 2 * u), F32), V((n, 2 * t), F32), V((R, C, h // 2, 2 * w), F32),
-        V((2 * t // PK, 128), F32), V((2 * t // PK, 128), F32), V((R, h // PK, 128), F32), V((C, h // PK, 128), F32),
-        V(ei.shape, F32), V(ie.shape, F32), V(ii.shape, F32), V(bd.shape, F32), V(ee.shape, F32),
-        V(lee.shape, F32), V(lei.shape, F32), V(lie.shape, F32), V(lii.shape, F32),
-        V((2, 2, t, t), F32), V((2, h, t), F32), V((h, q), F32), V((2, 2, tl, tl), F32), V((2, nl, tl), F32),
+        V((2, q, t), F32), V((2, q, t), F32), V((R, q, h), F32), V((C, q, h), F32),
+        V(ei.shape, F32), V(ie.shape, F32), V(ii.shape, F32), V(ee.shape, F32),
+        V(lee.shape, F32), V(lei.shape, F32), V((tl, nl), F32), V(lie.shape, F32), V(lii.shape, F32),
+        V((2, 2, t, t), F32), V((2, h, t), F32), V((q, h), F32), V((2, 2, tl, tl), F32), V((2, nl, tl), F32),
         V((n, n), F32), V((n, n), BF), V((n, n), BF), V((n, n), BF), V((n, n), BF), V((n, n), BF), V((n, n), BF),
         V((n, 2 * T), BF), V((n, 2 * T), BF), V((n, 2 * T), BF), V((n, 2 * T), BF),
         V((nl, 2 * TL), BF), V((nl, 2 * TL), BF), V((nl, 2 * TL), BF), V((nl, 2 * TL), BF),
@@ -455,12 +455,12 @@
     outs = (
         jax.ShapeDtypeStruct((2, 2, t, t), F32),
         jax.ShapeDtypeStruct((2, h, t), F32),
-        jax.ShapeDtypeStruct((h, q), F32),
+        jax.ShapeDtypeStruct((q, h), F32),
         jax.ShapeDtypeStruct((2, 2, tl, tl), F32),
         jax.ShapeDtypeStruct((2, nl, tl), F32),
     )
     got = pl.pallas_call(
-        functools.partial(kernel, R, C, M, PK),
+        functools.partial(kernel, R, C, M),
         out_shape=outs,
         in_specs=[pl.BlockSpec(memory_space=pl.ANY)] * 9,
         out_specs=[pl.BlockSpec(memory_space=pl.ANY)] * 5,
@@ -469,7 +469,7 @@
             collective_id=0, has_side_effects=True, vmem_limit_bytes=60 * 1024 * 1024),
         cost_estimate=pl.CostEstimate(flops=18 * n * n * t * 4, bytes_accessed=24 * t * t * 4, transcendentals=0),
     )(ee, ei, ie, ii, bd, lee, lei, lie, lii)
-    return got[0], got[1], got[2], got[3][None], got[4][None]
+    return got[0], got[1], got[2].T, got[3][None], got[4][None]
 
 
 def fits(R, C, shapes):
@@ -480,8 +480,7 @@
     boxes = shapes[5][0]
     return (
         R == C and R % 2 == 0 and C >= 3 and h == w == u and h % 16 == 0 and (2 * u) % 128 == 0 and t % 48 == 0
-        and 128 % q == 0 and h % (8 * (128 // q)) == 0 and (2 * t) % (8 * (128 // q)) == 0
-        and (128 // q) % 2 == 0 and tl % nl == 0 and nl % 16 == 0
+        and q % 16 == 0 and tl % nl == 0 and nl % 16 == 0
     )
 
 

time: 105 us -> 98.9 us (0.942)
  local copies, waits for them, and re-layouts: 19.1 us -> 10.9 us
  Pallas kernels: 84.6 us -> 86 us
    unnamed x16 -> x15, local copies, waits for them, and re-layouts: 19.1 us -> 10.9 us
    pallas_call x1, Pallas kernels: 84.6 us -> 86 us  [fused(): pl.pallas_call(functools.partial(kernel, R, C, M), out_shape=outs, in_spe...]
where the time goes in v2:
time: 98.9 us; the launch traced here: 97.6 us
  Pallas kernels  86 us (87%)
  local copies, waits for them, and re-layouts  10.9 us (11%)
    pallas_call x1, Pallas kernels, fused(): pl.pallas_call(functools.partial(kernel, R, C, M), out_shape=outs, in_spe...  86 us
    unnamed x15, local copies, waits for them, and re-layouts  10.9 us

profile of v2, /device:TPU:0, one launch (start us, length us, event | category | flops | bytes accessed | tf_op | source)
XLA Modules:
  0.0 97.6 jit_solution(3245069662627132836)
XLA Ops:
  0.6 86.0 %shard_map.128 = (f32[2,2,576,576]{3,2,1,0:T(8,128)}, f32[2,192,576]{2,1,0:T(8,128)}, f32[32,192]{1,0:T(8,128)}, f32[2,2,576,576]{3,2,1,0:T(8,128)}, f32[2,192,576]{2,1,0:T(8,128)}) custom-call(f32[2,576,576]{2,1,0:T(8,128)} %ee.1, f32[2,192,576]{2,1,0:T(8,128)} %bitcast.17, f32[2,192,576]{2,1,0:T(8,128)} %ie.1, f32[2,192,192]{2,1,0:T(8,128)} %ii.1, ...), custom_call_target="tpu_custom_call" | custom-call | flops 24461180928 | bytes 31850496 | tf_op jit(solution)/shard_map/pallas_call | solution.py:462
  86.6 0.0 slice-start
  86.6 0.0 copy-start.1
  86.6 0.0 copy-start.2
  86.6 0.0 slice-start.1
  86.6 5.8 %copy.19 = f32[2,2,576,576]{3,2,1,0:T(8,128)} copy(f32[2,2,576,576]{3,2,1,0:T(8,128)} %get-tuple-element.20) | data formatting | bytes 10616832
  92.5 0.0 copy-done.1
  92.5 0.9 copy.20
  93.4 0.0 copy-done.2
  93.4 0.6 copy.21
  94.0 0.0 slice-done
  94.0 0.0 slice-done.1
  94.0 0.0 copy-start
  94.0 2.6 %copy.22 = f32[1,2,2,576,576]{4,3,2,1,0:T(8,128)} copy(f32[1,2,2,576,576]{4,3,2,1,0:T(8,128)S(1)} %bitcast.13) | data formatting | bytes 10616832
  96.6 0.0 copy-done
  96.6 0.9 copy.23
  (1 shorter events, 0.0 us)
Async XLA Ops:
  86.6 7.4 %slice-start = ((s8[5898240]{0:T(1024)(128)(4,1)}), s8[4194304]{0:T(1024)(128)(4,1)S(1)}, s32[]{:S(2)}) async-start(s8[5898240]{0:T(1024)(128)(4,1)} %bitcast.11), calls=%async_computation | async-start | bytes 8388608
  86.6 5.8 %copy-start.1 = (f32[2,192,576]{2,1,0:T(8,128)S(1)}, f32[2,192,576]{2,1,0:T(8,128)}, u32[]{:S(2)}) copy-start(f32[2,192,576]{2,1,0:T(8,128)} %get-tuple-element.21) | copy-start | bytes 2654212
  86.6 6.8 %copy-start.2 = (f32[32,192]{1,0:T(8,128)S(1)}, f32[32,192]{1,0:T(8,128)}, u32[]{:S(2)}) copy-start(f32[32,192]{1,0:T(8,128)} %get-tuple-element.12) | copy-start | bytes 73732
  86.6 7.4 %slice-start.1 = ((s8[5898240]{0:T(1024)(128)(4,1)}), s8[1703936]{0:T(1024)(128)(4,1)S(1)}, s32[]{:S(2)}) async-start(s8[5898240]{0:T(1024)(128)(4,1)} %bitcast.11), calls=%async_computation.1 | async-start | bytes 3407872
  94.0 2.6 %copy-start = (f32[2,192,576]{2,1,0:T(8,128)S(1)}, f32[2,192,576]{2,1,0:T(8,128)}, u32[]{:S(2)}) copy-start(f32[2,192,576]{2,1,0:T(8,128)} %get-tuple-element.14) | copy-start | bytes 2654212
